TPU v7x, 256 devices: a whole 4x4x8 slice. The times are simulated.
256 devices in a mesh: dp: 2 (over core), head: 8 (over x, z_lo), ctx: 16 (over y, z_hi).
Axes of the slice: x: 4, y: 4, z: 8 (z_hi: 4, z_lo: 2; z = z_hi * 2 + z_lo), core: 2. Of those that a mesh axis runs over, the one named last changes fastest.
Arguments:
- query_states: bfloat16 [2, 16384, 32, 128], P('dp', 'ctx', 'head'), may hold values from -6 to 6
- key_states: bfloat16 [2, 16384, 8, 128], P('dp', 'ctx', 'head'), may hold values from -6 to 6
- value_states: bfloat16 [2, 16384, 8, 128], P('dp', 'ctx', 'head'), may hold values from -12 to 12
- gate_values: float32 [32], P('head'), may hold values from 0.1 to 0.9
- head_flags: int32 [32], P('head'), may hold values from 0 to 1, as said below
- output_grad: bfloat16 [2, 16384, 32, 128], P('dp', 'ctx', 'head'), may hold values from -16 to 16
Outputs:
- blended: bfloat16 [2, 16384, 32, 128], P('dp', 'ctx', 'head')
- gate_grad: float32 [32], replicated
Inputs may be any that keep to these rules, and one draw needn't show every extreme that they name: `head_flags`: exactly 1 of the 4 query heads of each key-value head have flag 1.
All inputs are finite; a program needn't handle non-finite values.
Results may differ from a plain program's by a relative error of at most 0.005.
Values may be sent and summed in bfloat16 or wider, within the bound.
No kernel may reach another device: no remote copies, remote signals or barrier semaphores. Data moves between devices by JAX's collectives and lax.ppermute only.
A program may use at most 64 MiB of HBM per device.

v0:
```python
import math
import jax
import jax.numpy as jnp
from jax import lax
from jax.sharding import PartitionSpec as P

RET = 1
SINK = 64
WINDOW = 2048


def from_behind(block, axis, distance):
    devices = range(lax.axis_size(axis))
    route = [(i - distance, i) for i in devices if i - distance in devices]
    return lax.ppermute(block, axis, route)


def empty_state(row_count, groups, heads, width):
    return (
        jnp.full((row_count, groups, heads), -jnp.inf, jnp.float32),
        jnp.zeros((row_count, groups, heads), jnp.float32),
        jnp.zeros((row_count, groups, heads, width), jnp.float32),
    )


def block_update(carried, query_block, key_rows, value_rows, allowed):
    running_max, running_sum, running_acc = carried
    scaling = 1.0 / math.sqrt(query_block.shape[-1])
    scores = (
        jnp.einsum("rgeh,kgh->rgek", query_block, key_rows, preferred_element_type=jnp.float32)
        * scaling
    )
    visible = allowed[:, None, None, :]
    scores = jnp.where(visible, scores, -jnp.inf)
    newest = jnp.maximum(running_max, jnp.max(scores, axis=-1))
    anchor = jnp.where(newest == -jnp.inf, 0.0, newest)
    factor = jnp.exp(running_max - anchor)
    weights = jnp.where(visible, jnp.exp(scores - anchor[..., None]), 0.0)
    running_sum = running_sum * factor + jnp.sum(weights, axis=-1)
    update = jnp.einsum(
        "rgek,kgh->rgeh",
        weights.astype(jnp.bfloat16),
        value_rows,
        preferred_element_type=jnp.float32,
    )
    running_acc = running_acc * factor[..., None] + update
    return (newest, running_sum, running_acc)


def sweep_blocks(carried, queries, positions, key_rows, value_rows, key_first, needed, allowed_fn):
    row_count = queries.shape[0]
    key_count = key_rows.shape[0]
    row_block = math.gcd(row_count, 512)
    key_block = math.gcd(key_count, 512)
    key_steps = key_count // key_block
    total_steps = row_count // row_block * key_steps

    def visit_block(counter, current):
        row_at = counter // key_steps * row_block
        key_at = counter % key_steps * key_block
        row_pos = lax.dynamic_slice_in_dim(positions, row_at, row_block)
        key_pos = key_first + key_at + jnp.arange(key_block, dtype=jnp.int32)

        def compute(present):
            portion = tuple(
                (lax.dynamic_slice_in_dim(member, row_at, row_block) for member in present)
            )
            renewed = block_update(
                portion,
                lax.dynamic_slice_in_dim(queries, row_at, row_block),
                lax.dynamic_slice_in_dim(key_rows, key_at, key_block),
                lax.dynamic_slice_in_dim(value_rows, key_at, key_block),
                allowed_fn(row_pos[:, None], key_pos[None, :]),
            )
            return tuple(
                (
                    lax.dynamic_update_slice_in_dim(member, fresh_part, row_at, 0)
                    for member, fresh_part in zip(present, renewed)
                )
            )

        def unchanged(present):
            return present

        return lax.cond(
            needed(row_pos[0], row_pos[row_block - 1], key_pos[0], key_pos[key_block - 1]),
            compute,
            unchanged,
            current,
        )

    return lax.fori_loop(0, total_steps, visit_block, carried)


def causal_needed(row_low, row_high, key_low, key_high):
    return key_low <= row_high


def causal_allowed(row_pos, key_pos):
    return key_pos <= row_pos


def window_needed(row_low, row_high, key_low, key_high):
    return (key_low <= row_high) & (key_high > row_low - WINDOW)


def window_allowed(row_pos, key_pos):
    return (key_pos >= 0) & (key_pos <= row_pos) & (row_pos - key_pos < WINDOW)


def sinks_needed(row_low, row_high, key_low, key_high):
    return (key_low < SINK) & (row_high - key_low >= WINDOW)


def sinks_allowed(row_pos, key_pos):
    return (key_pos < SINK) & (key_pos <= row_pos) & (row_pos - key_pos >= WINDOW)


def on_device(query_states, key_states, value_states, gate_values, head_flags, output_grad):
    tok_rows = query_states.shape[1]
    groups = key_states.shape[2]
    head_dim = key_states.shape[3]
    per_group = query_states.shape[2] // groups
    ctx_count = lax.axis_size("ctx")
    ctx_index = lax.axis_index("ctx")
    queries = query_states[0].reshape(tok_rows, groups, per_group, head_dim)
    stacked = jnp.stack([key_states[0], value_states[0]])
    marked = head_flags.reshape(groups, per_group)
    ordinal = jnp.cumsum(marked, axis=1) - 1
    slot_ids = jnp.arange(RET, dtype=jnp.int32)
    picker = ((marked[:, None, :] == 1) & (ordinal[:, None, :] == slot_ids[None, :, None])).astype(
        jnp.float32
    )
    chosen = jnp.einsum(
        "gre,tgeh->tgrh", picker.astype(jnp.bfloat16), queries, preferred_element_type=jnp.float32
    ).astype(jnp.bfloat16)
    own_pos = ctx_index * tok_rows + jnp.arange(tok_rows, dtype=jnp.int32)
    full_state = empty_state(tok_rows, groups, RET, head_dim)
    near_state = empty_state(tok_rows, groups, per_group, head_dim)
    portion = lax.all_gather(stacked, "ctx", axis=1, tiled=True)
    start = jnp.int32(0)
    full_now = sweep_blocks(
        full_state, chosen, own_pos, portion[0], portion[1], start, causal_needed, causal_allowed
    )
    head_rows = min(SINK, portion.shape[1])
    sink_part = portion[:, :head_rows]

    def with_sinks(present):
        return sweep_blocks(
            present,
            queries,
            own_pos,
            sink_part[0],
            sink_part[1],
            start,
            sinks_needed,
            sinks_allowed,
        )

    def without_sinks(present):
        return present

    near_now = lax.cond(start < SINK, with_sinks, without_sinks, near_state)
    near_state = near_now
    reach_depth = min((WINDOW - 1) // tok_rows + 1, ctx_count - 1)
    earlier = [from_behind(stacked, "ctx", distance) for distance in range(reach_depth, 0, -1)]
    near_keys = jnp.concatenate(earlier + [stacked], axis=1)
    near_state = sweep_blocks(
        near_state,
        queries,
        own_pos,
        near_keys[0],
        near_keys[1],
        (ctx_index - reach_depth) * tok_rows,
        window_needed,
        window_allowed,
    )
    full_out = full_now[2] / full_now[1][..., None]
    near_out = near_state[2] / near_state[1][..., None]
    full_heads = jnp.einsum("gre,tgrh->tgeh", picker, full_out, precision=lax.Precision.HIGHEST)
    gate_cols = gate_values.reshape(groups, per_group)[None, :, :, None]
    retrieval = (marked == 1)[None, :, :, None]
    mixed = jnp.where(retrieval, gate_cols * full_heads + (1.0 - gate_cols) * near_out, near_out)
    blended = mixed.astype(jnp.bfloat16).reshape(1, tok_rows, groups * per_group, head_dim)
    grad_rows = output_grad[0].reshape(tok_rows, groups, per_group, head_dim).astype(jnp.float32)
    local_terms = jnp.sum(grad_rows * (full_heads - near_out), axis=(0, 3)) * marked.astype(
        jnp.float32
    )
    heads_dev = groups * per_group
    padded = lax.dynamic_update_slice_in_dim(
        jnp.zeros((heads_dev * lax.axis_size("head"),), jnp.float32),
        local_terms.reshape(heads_dev),
        lax.axis_index("head") * heads_dev,
        0,
    )
    totals = lax.psum(padded, ("dp", "head", "ctx"))
    normalizer = 1.0 / math.sqrt(
        lax.axis_size("dp") * query_states.shape[0] * tok_rows * ctx_count * head_dim
    )
    return (blended, totals * normalizer)


def solution(mesh):
    return jax.shard_map(
        on_device,
        mesh=mesh,
        in_specs=(
            P("dp", "ctx", "head", None),
            P("dp", "ctx", "head", None),
            P("dp", "ctx", "head", None),
            P("head"),
            P("head"),
            P("dp", "ctx", "head", None),
        ),
        out_specs=(P("dp", "ctx", "head", None), P()),
        check_vma=False,
    )
```

profile of v0, /device:TPU:1, one launch (start us, length us, event | category | flops | bytes accessed | tf_op | source)
XLA Modules:
  0.0 829.5 jit_solution(2054756737701288816)
XLA Ops:
  10.1 5.8 collective-permute-start.1
  15.9 7.8 collective-permute-start
  31.2 24.1 %collective-permute-done = bf16[2,1024,1,128]{3,1,2,0:T(8,128)(2,1)} collective-permute-done((bf16[2,1024,1,128]{3,1,2,0:T(8,128)(2,1)}, bf16[2,1024,1,128]{3,1,2,0:T(8,128)(2,1)}, u32[]{:S(2)}, u32[]{:S(2)}) %collective-permute-start) | collective-permute-done | bytes 524320 | tf_op jit(solution)/shard_map/ppermute | solution.py:15
  58.6 96.1 %all-gather.2.cloned.1.call-done = bf16[2,16384,1,128]{3,1,2,0:T(8,128)(2,1)} async-done(((bf16[2,1024,1,128]{3,1,2,0:T(8,128)(2,1)}), bf16[2,16384,1,128]{3,1,2,0:T(8,128)(2,1)}) %all-gather.2.cloned.1.call-update) | async-done | bytes 8388624 | tf_op jit(solution)/shard_map/all_gather | solution.py:140
  154.6 5.7 slice_bitcast_fusion
  160.4 183.1 %while.58 = (s32[]{:T(128)}, f32[1024,1,1]{0,2,1:T(1,128)S(1)}, f32[1024,1,1]{0,2,1:T(1,128)S(1)}, f32[1024,1,1,128]{0,3,2,1:T(8,128)S(1)}, s32[1024]{0:T(1024)S...) while((s32[]{:T(128)}, f32[1024,1,1]{0,2,1:T(1,128)S(1)}, ...), condition=%wide.region_6.7_spmd, body=%wide.region_1.6_spmd.sunk | while | flops 137498128 | bytes 4645472 | solution.py:92
  350.4 158.5 %while.60 = (s32[]{:T(128)}, f32[1024,1,4]{0,2,1:T(4,128)S(1)}, f32[1024,1,4]{0,2,1:T(4,128)S(1)}, f32[1024,1,4,128]{0,3,2,1:T(8,128)}, s32[]{:T(128)}, /*index=...) while((s32[]{:T(128)}, f32[1024,1,4]{0,2,1:T(4,128)S(1)}, ...), condition=%wide.region_18.19_spmd, body=%wide.region_13.18_spmd.sunk | while | flops 552356864 | bytes 27178672 | solution.py:92
  353.4 12.6 %conditional.8 = ((f32[1024,1,4]{0,2,1:T(4,128)S(1)}, f32[1024,1,4]{0,2,1:T(4,128)S(1)}, f32[1024,1,4,128]{0,3,2,1:T(8,128)})) conditional(s32[]{:T(128)} %bitcast.205, (f32[1024,1,4]{0,2,1:T(4,128)S(1)}, f32[1024,1,4]{0,2,1:T(4,128)S(1)}, f32[1024,1,4,128]{0,3,2,1:T(8,128)}) %tuple.164, (s32[]{:T(128)}, f32[1024,1,4]{0,2,1:T(4,128)S(1)}, ...), branch_computations={%region_14.14_spmd, %region_15.17_spmd} | conditional | flops 552356352 | bytes 27172004 | solution.py:85
  360.3 5.7 dynamic_update_slice.31
  369.1 12.6 %conditional.8 = ((f32[1024,1,4]{0,2,1:T(4,128)S(1)}, f32[1024,1,4]{0,2,1:T(4,128)S(1)}, f32[1024,1,4,128]{0,3,2,1:T(8,128)})) conditional(s32[]{:T(128)} %bitcast.205, (f32[1024,1,4]{0,2,1:T(4,128)S(1)}, f32[1024,1,4]{0,2,1:T(4,128)S(1)}, f32[1024,1,4,128]{0,3,2,1:T(8,128)}) %tuple.164, (s32[]{:T(128)}, f32[1024,1,4]{0,2,1:T(4,128)S(1)}, ...), branch_computations={%region_14.14_spmd, %region_15.17_spmd} | conditional | flops 552356352 | bytes 27172004 | solution.py:85
  376.0 5.7 dynamic_update_slice.31
  384.8 12.6 %conditional.8 = ((f32[1024,1,4]{0,2,1:T(4,128)S(1)}, f32[1024,1,4]{0,2,1:T(4,128)S(1)}, f32[1024,1,4,128]{0,3,2,1:T(8,128)})) conditional(s32[]{:T(128)} %bitcast.205, (f32[1024,1,4]{0,2,1:T(4,128)S(1)}, f32[1024,1,4]{0,2,1:T(4,128)S(1)}, f32[1024,1,4,128]{0,3,2,1:T(8,128)}) %tuple.164, (s32[]{:T(128)}, f32[1024,1,4]{0,2,1:T(4,128)S(1)}, ...), branch_computations={%region_14.14_spmd, %region_15.17_spmd} | conditional | flops 552356352 | bytes 27172004 | solution.py:85
  391.6 5.7 dynamic_update_slice.31
  400.4 12.6 %conditional.8 = ((f32[1024,1,4]{0,2,1:T(4,128)S(1)}, f32[1024,1,4]{0,2,1:T(4,128)S(1)}, f32[1024,1,4,128]{0,3,2,1:T(8,128)})) conditional(s32[]{:T(128)} %bitcast.205, (f32[1024,1,4]{0,2,1:T(4,128)S(1)}, f32[1024,1,4]{0,2,1:T(4,128)S(1)}, f32[1024,1,4,128]{0,3,2,1:T(8,128)}) %tuple.164, (s32[]{:T(128)}, f32[1024,1,4]{0,2,1:T(4,128)S(1)}, ...), branch_computations={%region_14.14_spmd, %region_15.17_spmd} | conditional | flops 552356352 | bytes 27172004 | solution.py:85
  407.3 5.7 dynamic_update_slice.31
  416.1 12.6 %conditional.8 = ((f32[1024,1,4]{0,2,1:T(4,128)S(1)}, f32[1024,1,4]{0,2,1:T(4,128)S(1)}, f32[1024,1,4,128]{0,3,2,1:T(8,128)})) conditional(s32[]{:T(128)} %bitcast.205, (f32[1024,1,4]{0,2,1:T(4,128)S(1)}, f32[1024,1,4]{0,2,1:T(4,128)S(1)}, f32[1024,1,4,128]{0,3,2,1:T(8,128)}) %tuple.164, (s32[]{:T(128)}, f32[1024,1,4]{0,2,1:T(4,128)S(1)}, ...), branch_computations={%region_14.14_spmd, %region_15.17_spmd} | conditional | flops 552356352 | bytes 27172004 | solution.py:85
  423.0 5.7 dynamic_update_slice.31
  438.0 11.7 %conditional.8 = ((f32[1024,1,4]{0,2,1:T(4,128)S(1)}, f32[1024,1,4]{0,2,1:T(4,128)S(1)}, f32[1024,1,4,128]{0,3,2,1:T(8,128)})) conditional(s32[]{:T(128)} %bitcast.205, (f32[1024,1,4]{0,2,1:T(4,128)S(1)}, f32[1024,1,4]{0,2,1:T(4,128)S(1)}, f32[1024,1,4,128]{0,3,2,1:T(8,128)}) %tuple.164, (s32[]{:T(128)}, f32[1024,1,4]{0,2,1:T(4,128)S(1)}, ...), branch_computations={%region_14.14_spmd, %region_15.17_spmd} | conditional | flops 552356352 | bytes 27172004 | solution.py:85
  452.8 11.8 %conditional.8 = ((f32[1024,1,4]{0,2,1:T(4,128)S(1)}, f32[1024,1,4]{0,2,1:T(4,128)S(1)}, f32[1024,1,4,128]{0,3,2,1:T(8,128)})) conditional(s32[]{:T(128)} %bitcast.205, (f32[1024,1,4]{0,2,1:T(4,128)S(1)}, f32[1024,1,4]{0,2,1:T(4,128)S(1)}, f32[1024,1,4,128]{0,3,2,1:T(8,128)}) %tuple.164, (s32[]{:T(128)}, f32[1024,1,4]{0,2,1:T(4,128)S(1)}, ...), branch_computations={%region_14.14_spmd, %region_15.17_spmd} | conditional | flops 552356352 | bytes 27172004 | solution.py:85
  467.6 11.7 %conditional.8 = ((f32[1024,1,4]{0,2,1:T(4,128)S(1)}, f32[1024,1,4]{0,2,1:T(4,128)S(1)}, f32[1024,1,4,128]{0,3,2,1:T(8,128)})) conditional(s32[]{:T(128)} %bitcast.205, (f32[1024,1,4]{0,2,1:T(4,128)S(1)}, f32[1024,1,4]{0,2,1:T(4,128)S(1)}, f32[1024,1,4,128]{0,3,2,1:T(8,128)}) %tuple.164, (s32[]{:T(128)}, f32[1024,1,4]{0,2,1:T(4,128)S(1)}, ...), branch_computations={%region_14.14_spmd, %region_15.17_spmd} | conditional | flops 552356352 | bytes 27172004 | solution.py:85
  482.4 11.8 %conditional.8 = ((f32[1024,1,4]{0,2,1:T(4,128)S(1)}, f32[1024,1,4]{0,2,1:T(4,128)S(1)}, f32[1024,1,4,128]{0,3,2,1:T(8,128)})) conditional(s32[]{:T(128)} %bitcast.205, (f32[1024,1,4]{0,2,1:T(4,128)S(1)}, f32[1024,1,4]{0,2,1:T(4,128)S(1)}, f32[1024,1,4,128]{0,3,2,1:T(8,128)}) %tuple.164, (s32[]{:T(128)}, f32[1024,1,4]{0,2,1:T(4,128)S(1)}, ...), branch_computations={%region_14.14_spmd, %region_15.17_spmd} | conditional | flops 552356352 | bytes 27172004 | solution.py:85
  497.2 11.7 %conditional.8 = ((f32[1024,1,4]{0,2,1:T(4,128)S(1)}, f32[1024,1,4]{0,2,1:T(4,128)S(1)}, f32[1024,1,4,128]{0,3,2,1:T(8,128)})) conditional(s32[]{:T(128)} %bitcast.205, (f32[1024,1,4]{0,2,1:T(4,128)S(1)}, f32[1024,1,4]{0,2,1:T(4,128)S(1)}, f32[1024,1,4,128]{0,3,2,1:T(8,128)}) %tuple.164, (s32[]{:T(128)}, f32[1024,1,4]{0,2,1:T(4,128)S(1)}, ...), branch_computations={%region_14.14_spmd, %region_15.17_spmd} | conditional | flops 552356352 | bytes 27172004 | solution.py:85
  511.2 6.3 fusion.69
  517.7 304.5 %psum.7 = f32[32]{0:T(128)S(1)} all-reduce(f32[32]{0:T(128)S(1)} %multiply_dynamic-update-slice_fusion), channel_id=1, replica_groups=mesh['dp'=2,'head'=8,'ctx'=16] {'dp','head','ctx'}, use_global_device_ids=true, to_apply=%region_20.21 | all-reduce | flops 32 | bytes 256 | tf_op jit(solution)/shard_map/psum | solution.py:196
  (560 shorter events, 232.3 us)
Async XLA Ops:
  7.2 20.2 %copy-start.4 = (bf16[1,1024,4,128]{3,2,1,0:T(4,128)(2,1)S(1)}, bf16[1,1024,4,128]{3,2,1,0:T(4,128)(2,1)}, u32[]{:S(2)}) copy-start(bf16[1,1024,4,128]{3,2,1,0:T(4,128)(2,1)} %param.18) | copy-start | bytes 3145732
  7.2 147.5 %all-gather.2.cloned.1.call-start = ((), (), s32[]{:S(2)}) async-start(), calls=%async_computation | async-start | bytes 8912896 | tf_op jit(solution)/shard_map/all_gather | solution.py:140
  9.3 0.8 copy-start.1
  10.1 21.1 %collective-permute-start.1 = (bf16[2,1024,1,128]{3,1,2,0:T(8,128)(2,1)}, bf16[2,1024,1,128]{3,1,2,0:T(8,128)(2,1)S(1)}, u32[]{:S(2)}, u32[]{:S(2)}) collective-permute-start(bf16[2,1024,1,128]{3,1,2,0:T(8,128)(2,1)} %copy-done.1), channel_id=1, source_target_pairs={{0,1},{1,2},{2,3},{3,4},{4,5},{5,6},{6,7},{7,8},{8,9},{9,10},{10,1... | collective-permute-start | bytes 1572872 | tf_op jit(solution)/shard_map/ppermute | solution.py:15
  15.9 39.4 %collective-permute-start = (bf16[2,1024,1,128]{3,1,2,0:T(8,128)(2,1)}, bf16[2,1024,1,128]{3,1,2,0:T(8,128)(2,1)}, u32[]{:S(2)}, u32[]{:S(2)}) collective-permute-start(bf16[2,1024,1,128]{3,1,2,0:T(8,128)(2,1)} %copy-done.1), channel_id=1, source_target_pairs={{0,2},{1,3},{2,4},{3,5},{4,6},{5,7},{6,8},{7,9},{8,10},{9,11},{10,... | collective-permute-start | bytes 1572872 | tf_op jit(solution)/shard_map/ppermute | solution.py:15
  25.8 29.4 %copy-start.2 = (bf16[2,1024,1,128]{3,1,2,0:T(8,128)(2,1)S(1)}, bf16[2,1024,1,128]{3,1,2,0:T(8,128)(2,1)}, u32[]{:S(2)}) copy-start(bf16[2,1024,1,128]{3,1,2,0:T(8,128)(2,1)} %copy-done.1) | copy-start | bytes 1572868
  355.7 1.6 copy-start
  371.4 1.6 copy-start
  387.0 1.6 copy-start
  402.7 1.6 copy-start
  418.4 1.6 copy-start
  440.3 1.6 copy-start
  455.1 1.6 copy-start
  469.9 1.6 copy-start
  484.7 1.6 copy-start
  499.5 1.6 copy-start
  508.9 2.3 copy-start.3
  508.9 2.3 copy-start.6
  511.2 6.4 copy-start.5
Sparse Core Ops, SparseCore 0:
  10.5 144.0 all-gather.1
where the time goes:
time: 836 us; the launch traced here: 829 us
  blocking collectives  304 us (36%)
  local copies, waits for them, and re-layouts  177 us (21%)
  waiting for transfers between devices  123 us (15%)
  loops' own time  119 us (14%)
  matrix products  50 us (6%)
  other arithmetic  27.9 us (3%)
  between operations  14.2 us (2%)
  starting transfers between devices  13.6 us (2%)
    psum x1, blocking collectives, on_device(): totals = lax.psum(padded, ('dp', 'head', 'ctx'))  304 us
    another operation x3, loops' own time, sweep_blocks(): return lax.fori_loop(0, total_steps, visit_block, carried)  117 us
    all_gather x1, waiting for transfers between devices, on_device(): portion = lax.all_gather(stacked, 'ctx', axis=1, tiled=True)  96.1 us
    dynamic_update_slice x39, local copies, waits for them, and re-layouts, compute(): lax.dynamic_update_slice_in_dim(member, fresh_part, row_at, 0)  60.7 us
    slice x66, local copies, waits for them, and re-layouts, visit_block(): row_pos[row_block - 1]  42.8 us
    slice x64, local copies, waits for them, and re-layouts, visit_block(): key_pos[0]  37.7 us
    ppermute x2, waiting for transfers between devices, from_behind(): return lax.ppermute(block, axis, route)  27.2 us
    dot_general x13, matrix products, block_update(): jnp.einsum('rgek,kgh->rgeh', weights.astype(jnp.bfloat16), value_rows, pr...  26.8 us
  transfers between devices with their start and end apart: 3, of which 3 were waited for; matrix products, arithmetic and copies ran while one was open for 1% of the time, Pallas kernels for 0%

commit v1 on v0

--- a/solution.py
+++ b/solution.py
@@ -1,3 +1,4 @@
+import functools
 import math
 import jax
 import jax.numpy as jnp
@@ -7,6 +8,15 @@
 RET = 1
 SINK = 64
 WINDOW = 2048
+
+
+def _match_ports(shard_in, which_axis):
+    x_next = jax.lax.all_gather(shard_in, which_axis)
+    wide_out = jnp.sum(x_next, axis=0)
+    return wide_out
+
+
+state_put = functools.partial(_match_ports, which_axis=("dp", "head", "ctx"))
 
 
 def from_behind(block, axis, distance):
@@ -193,7 +203,7 @@
         lax.axis_index("head") * heads_dev,
         0,
     )
-    totals = lax.psum(padded, ("dp", "head", "ctx"))
+    totals = state_put(padded)
     normalizer = 1.0 / math.sqrt(
         lax.axis_size("dp") * query_states.shape[0] * tok_rows * ctx_count * head_dim
     )

time: 836 us -> 1420 us (1.70)
  the two profiles are of different devices: /device:TPU:1 before, /device:TPU:36 now
where the time goes in v1:
time: 1420 us; the launch traced here: 1410 us
  blocking collectives  879 us (62%)
  local copies, waits for them, and re-layouts  177 us (12%)
  waiting for transfers between devices  129 us (9%)
  loops' own time  119 us (8%)
  matrix products  50 us (4%)
  other arithmetic  28.1 us (2%)
    all_gather x1, blocking collectives, _match_ports(): x_next = jax.lax.all_gather(shard_in, which_axis)  879 us
    another operation x3, loops' own time, sweep_blocks(): return lax.fori_loop(0, total_steps, visit_block, carried)  117 us
    all_gather x1, waiting for transfers between devices, on_device(): portion = lax.all_gather(stacked, 'ctx', axis=1, tiled=True)  84.6 us
    dynamic_update_slice x39, local copies, waits for them, and re-layouts, compute(): lax.dynamic_update_slice_in_dim(member, fresh_part, row_at, 0)  60.7 us
    ppermute x2, waiting for transfers between devices, from_behind(): return lax.ppermute(block, axis, route)  44.5 us
    slice x66, local copies, waits for them, and re-layouts, visit_block(): row_pos[row_block - 1]  42.8 us
    slice x64, local copies, waits for them, and re-layouts, visit_block(): key_pos[0]  37.7 us
  transfers between devices with their start and end apart: 3, of which 2 were waited for; matrix products, arithmetic and copies ran while one was open for 1% of the time, Pallas kernels for 0%

profile of v1, /device:TPU:36, one launch (start us, length us, event | category | flops | bytes accessed | tf_op | source)
XLA Modules:
  0.0 1409.7 jit_solution(3738678103614482157)
XLA Ops:
  10.1 5.2 collective-permute-start.1
  15.3 7.2 collective-permute-start
  26.9 44.5 %collective-permute-done.1 = bf16[2,1024,1,128]{3,1,2,0:T(8,128)(2,1)S(1)} collective-permute-done((bf16[2,1024,1,128]{3,1,2,0:T(8,128)(2,1)}, bf16[2,1024,1,128]{3,1,2,0:T(8,128)(2,1)S(1)}, u32[]{:S(2)}, u32[]{:S(2)}) %collective-permute-start.1) | collective-permute-done | bytes 524320 | tf_op jit(solution)/shard_map/ppermute | solution.py:25
  74.8 84.6 %all-gather.3.cloned.1.call-done = bf16[2,16384,1,128]{3,1,2,0:T(8,128)(2,1)} async-done(((bf16[2,1024,1,128]{3,1,2,0:T(8,128)(2,1)}), bf16[2,16384,1,128]{3,1,2,0:T(8,128)(2,1)}) %all-gather.3.cloned.1.call-update) | async-done | bytes 8388624 | tf_op jit(solution)/shard_map/all_gather | solution.py:150
  159.4 5.7 slice_bitcast_fusion
  165.2 183.1 %while.58 = (s32[]{:T(128)}, f32[1024,1,1]{0,2,1:T(1,128)S(1)}, f32[1024,1,1]{0,2,1:T(1,128)S(1)}, f32[1024,1,1,128]{0,3,2,1:T(8,128)S(1)}, s32[1024]{0:T(1024)S...) while((s32[]{:T(128)}, f32[1024,1,1]{0,2,1:T(1,128)S(1)}, ...), condition=%wide.region_6.7_spmd, body=%wide.region_1.6_spmd.sunk | while | flops 137498128 | bytes 4645472 | solution.py:102
  355.2 158.5 %while.60 = (s32[]{:T(128)}, f32[1024,1,4]{0,2,1:T(4,128)S(1)}, f32[1024,1,4]{0,2,1:T(4,128)S(1)}, f32[1024,1,4,128]{0,3,2,1:T(8,128)}, s32[]{:T(128)}, /*index=...) while((s32[]{:T(128)}, f32[1024,1,4]{0,2,1:T(4,128)S(1)}, ...), condition=%wide.region_18.19_spmd, body=%wide.region_13.18_spmd.sunk | while | flops 552356864 | bytes 27178672 | solution.py:102
  358.2 12.6 conditional.8
  365.1 5.7 dynamic_update_slice.32
  373.9 12.6 conditional.8
  380.7 5.7 dynamic_update_slice.32
  389.5 12.6 conditional.8
  396.4 5.7 dynamic_update_slice.32
  405.2 12.6 conditional.8
  412.1 5.7 dynamic_update_slice.32
  420.8 12.6 conditional.8
  427.7 5.7 dynamic_update_slice.32
  442.8 11.7 conditional.8
  457.6 11.8 conditional.8
  472.4 11.7 conditional.8
  487.1 11.8 conditional.8
  501.9 11.7 conditional.8
  516.0 6.3 fusion.69
  522.6 879.4 %all-gather = f32[256,1,32]{2,1,0:T(1,128)S(1)} all-gather(f32[1,1,32]{2,1,0:T(1,128)S(1)} %dynamic_update_slice.35), channel_id=1, replica_groups=mesh['dp'=2,'head'=8,'ctx'=16] {'dp','head','ctx'}, dimensions={0}, use_global_device_ids=true | all-gather | bytes 32896 | tf_op jit(solution)/shard_map/all_gather | solution.py:14
  (562 shorter events, 229.6 us)
Async XLA Ops:
  7.2 19.0 %copy-start.4 = (bf16[1,1024,4,128]{3,2,1,0:T(4,128)(2,1)S(1)}, bf16[1,1024,4,128]{3,2,1,0:T(4,128)(2,1)}, u32[]{:S(2)}) copy-start(bf16[1,1024,4,128]{3,2,1,0:T(4,128)(2,1)} %param.18) | copy-start | bytes 3145732
  7.2 152.2 %all-gather.3.cloned.1.call-start = ((), (), s32[]{:S(2)}) async-start(), calls=%async_computation | async-start | bytes 8912896 | tf_op jit(solution)/shard_map/all_gather | solution.py:150
  9.3 0.8 copy-start.1
  10.1 61.4 %collective-permute-start.1 = (bf16[2,1024,1,128]{3,1,2,0:T(8,128)(2,1)}, bf16[2,1024,1,128]{3,1,2,0:T(8,128)(2,1)S(1)}, u32[]{:S(2)}, u32[]{:S(2)}) collective-permute-start(bf16[2,1024,1,128]{3,1,2,0:T(8,128)(2,1)} %copy-done.1), channel_id=1, source_target_pairs={{0,1},{1,2},{2,3},{3,4},{4,5},{5,6},{6,7},{7,8},{8,9},{9,10},{10,1... | collective-permute-start | bytes 1572872 | tf_op jit(solution)/shard_map/ppermute | solution.py:25
  15.3 56.1 %collective-permute-start = (bf16[2,1024,1,128]{3,1,2,0:T(8,128)(2,1)}, bf16[2,1024,1,128]{3,1,2,0:T(8,128)(2,1)}, u32[]{:S(2)}, u32[]{:S(2)}) collective-permute-start(bf16[2,1024,1,128]{3,1,2,0:T(8,128)(2,1)} %copy-done.1), channel_id=1, source_target_pairs={{0,2},{1,3},{2,4},{3,5},{4,6},{5,7},{6,8},{7,9},{8,10},{9,11},{10,... | collective-permute-start | bytes 1572872 | tf_op jit(solution)/shard_map/ppermute | solution.py:25
  24.7 46.8 %copy-start.2 = (bf16[2,1024,1,128]{3,1,2,0:T(8,128)(2,1)S(1)}, bf16[2,1024,1,128]{3,1,2,0:T(8,128)(2,1)}, u32[]{:S(2)}) copy-start(bf16[2,1024,1,128]{3,1,2,0:T(8,128)(2,1)} %copy-done.1) | copy-start | bytes 1572868
  360.5 1.6 copy-start
  376.2 1.6 copy-start
  391.8 1.6 copy-start
  407.5 1.6 copy-start
  423.2 1.6 copy-start
  445.1 1.6 copy-start
  459.9 1.6 copy-start
  474.7 1.6 copy-start
  489.5 1.6 copy-start
  504.2 1.6 copy-start
  513.7 2.3 copy-start.3
  513.7 2.3 copy-start.5
  515.9 6.4 copy-start.6
Sparse Core Ops, SparseCore 0:
  10.5 148.8 all-gather.2
